TPU v7x, 512 devices: a whole 4x4x16 slice. The times are simulated.
512 devices in a mesh: seq: 128 (over z, x, core), head: 4 (over y).
Axes of the slice: x: 4, y: 4, z: 16, core: 2. Of those that a mesh axis runs over, the one named last changes fastest.
Arguments:
- queries: bfloat16 [32768, 512], P('seq', 'head'), may hold values from -16 to 16
- keys: bfloat16 [32768, 512], P('seq', 'head'), may hold values from -16 to 16
- values: bfloat16 [32768, 512], P('seq', 'head'), may hold values from -16 to 16
- out_weight: bfloat16 [512, 512], replicated, may hold values from -0.5 to 0.5
Outputs:
- mixed: bfloat16 [32768, 512], P(('seq', 'head'))
All inputs are finite; a program needn't handle non-finite values.
Results may differ from a plain program's by a relative error of at most 0.00185.
The roundings to bfloat16 on the way count: a program that leaves them out, or rounds other values in their place, can miss the bound.
Values may be sent and summed in bfloat16 or wider, within the bound.
A program may use at most 128 MiB of HBM per device.

v0:
```python
import math

import jax
import jax.numpy as jnp
from jax import lax
from jax.sharding import PartitionSpec as P

HD = 64
LEAF = 128


def extended_2(cells, sides, width):
    for axis, dim in sides:
        count = lax.axis_size(axis)
        ends = count - 1
        head = lax.slice_in_dim(cells, 0, width, axis=dim)
        tail = lax.slice_in_dim(cells, cells.shape[dim] - width, cells.shape[dim], axis=dim)
        cells = jnp.concatenate(
            [
                lax.ppermute(tail, axis, [(i, (i + 1) % count) for i in range(ends)]),
                cells,
                lax.ppermute(head, axis, [((i + 1) % count, i) for i in range(ends)]),
            ],
            axis=dim,
        )
    return cells


def as_sent(x):

    def short(part):
        return part.astype(jnp.bfloat16) if part.dtype == jnp.float32 else part

    return jax.tree.map(short, x)


def average_pairs(stacked):
    widened = stacked.astype(jnp.float32).reshape(2, stacked.shape[1] // 2, 2, stacked.shape[2])
    return (0.5 * (widened[:, :, 0] + widened[:, :, 1])).astype(jnp.bfloat16)


def near_set(leaf, extended, seq_index, blocks_dev, seq_size):
    positions = jnp.arange(LEAF, dtype=jnp.int32)
    upper_half = positions >= LEAF // 2
    global_leaf = seq_index * blocks_dev + leaf
    all_blocks = seq_size * blocks_dev
    key_parts = [lax.dynamic_slice_in_dim(extended[0], leaf * LEAF, 3 * LEAF, 1)]
    neighbour = global_leaf - 1 + jnp.arange(3 * LEAF, dtype=jnp.int32) // LEAF
    valid_parts = [(neighbour >= 0) & (neighbour < all_blocks)]
    local_block = leaf >> 1
    global_block = global_leaf >> 1
    parity = global_leaf >> 0 & 1
    level_blocks = all_blocks >> 1
    key_parts.append(lax.dynamic_slice_in_dim(extended[1], local_block * LEAF, LEAF, 1))
    key_parts.append(lax.dynamic_slice_in_dim(extended[1], (local_block + 2) * LEAF, LEAF, 1))
    valid_parts.append((global_block >= 1) & jnp.logical_not(upper_half & (parity == 0)))
    valid_parts.append(
        (global_block + 1 < level_blocks)
        & jnp.logical_not(jnp.logical_not(upper_half) & (parity == 1))
    )
    return (jnp.concatenate(key_parts, axis=1), jnp.concatenate(valid_parts, axis=0))


def shards(queries, keys, values, out_weight):
    tok_count = queries.shape[0]
    width = queries.shape[1]
    seq_size = lax.axis_size("seq")
    seq_index = lax.axis_index("seq")
    blocks_dev = tok_count // LEAF
    near_count = blocks_dev.bit_length() - 1
    far_count = max(0, seq_size.bit_length() - 2)
    scale = 1.0 / math.sqrt(HD)
    positions = jnp.arange(LEAF, dtype=jnp.int32)
    upper_half = positions >= LEAF // 2
    local = [jnp.stack([keys, values], axis=0)]
    local.append(average_pairs(local[-1]))
    extended = [extended_2(stacked, (("seq", 1),), LEAF) for stacked in local]
    own_block = local[near_count]
    far_pairs = []
    far_valid = []
    everything = lax.all_gather(own_block, "seq", axis=1, tiled=True)
    for level_far in range(1, far_count + 1):
        everything = average_pairs(everything)
        group = seq_index >> level_far
        padded = jnp.pad(everything, ((0, 0), (LEAF, LEAF), (0, 0)))
        lower = lax.dynamic_slice_in_dim(padded, group * LEAF, LEAF, 1)
        upper = lax.dynamic_slice_in_dim(padded, (group + 2) * LEAF, LEAF, 1)
        far_pairs.append(jnp.concatenate([lower, upper], axis=1))
    for level_far in range(1, far_count + 1):
        group = seq_index >> level_far
        parity = seq_index >> level_far - 1 & 1
        far_valid.append((group >= 1) & jnp.logical_not(upper_half & (parity == 0)))
        far_valid.append(
            (group + 1 < seq_size >> level_far)
            & jnp.logical_not(jnp.logical_not(upper_half) & (parity == 1))
        )
    far_keys = jnp.concatenate(far_pairs, axis=1)
    far_mask = jnp.concatenate(far_valid, axis=0)
    leaves_step = min(blocks_dev, max(1, 512 // LEAF))
    step_count = blocks_dev // leaves_step

    def attend(step):
        leaves = step * leaves_step + jnp.arange(leaves_step, dtype=jnp.int32)
        near_keys, near_mask = jax.vmap(
            lambda leaf: near_set(leaf, extended, seq_index, blocks_dev, seq_size)
        )(leaves)
        query_block = queries.reshape(leaves_step, LEAF, width)
        head_outputs = []
        for head_number in range(width // HD):
            low_col = head_number * HD
            high_col = low_col + HD
            near_scores = (
                jnp.einsum(
                    "nhs,nos->nho",
                    query_block[:, :, low_col:high_col],
                    near_keys[:, 0, :, low_col:high_col],
                    preferred_element_type=jnp.float32,
                )
                * scale
            )
            near_scores = jnp.where(near_mask[:, None, :], near_scores, -jnp.inf)
            peak = jnp.max(near_scores, axis=-1, keepdims=True)
            far_scores = (
                jnp.einsum(
                    "qs,os->qo",
                    queries[:, low_col:high_col],
                    far_keys[0, :, low_col:high_col],
                    preferred_element_type=jnp.float32,
                )
                * scale
            )
            far_scores = far_scores.reshape(leaves_step, LEAF, far_scores.shape[-1])
            far_scores = jnp.where(far_mask[None, None, :], far_scores, -jnp.inf)
            peak = jnp.maximum(peak, jnp.max(far_scores, axis=-1, keepdims=True))
            near_weights = jnp.exp(near_scores - peak)
            total = jnp.sum(near_weights, axis=-1)
            numer = jnp.einsum(
                "fkm,fmp->fkp",
                near_weights.astype(jnp.bfloat16),
                near_keys[:, 1, :, low_col:high_col],
                preferred_element_type=jnp.float32,
            )
            far_weights = jnp.exp(far_scores - peak)
            total = total + jnp.sum(far_weights, axis=-1)
            far_rounded = far_weights.astype(jnp.bfloat16).reshape(
                leaves_step * LEAF, far_weights.shape[-1]
            )
            far_numer = jnp.dot(
                far_rounded, far_keys[1, :, low_col:high_col], preferred_element_type=jnp.float32
            )
            numer = numer + far_numer.reshape(leaves_step, LEAF, HD)
            head_outputs.append((numer / total[..., None]).astype(jnp.bfloat16))
        return jnp.concatenate(head_outputs, axis=-1).reshape(leaves_step * LEAF, width)

    attended = lax.map(attend, jnp.arange(step_count, dtype=jnp.int32)).reshape(tok_count, width)
    gathered_rows = lax.all_to_all(
        as_sent(attended), "head", split_axis=0, concat_axis=1, tiled=True
    ).astype(attended.dtype)
    return jnp.dot(gathered_rows, out_weight, preferred_element_type=jnp.float32).astype(
        jnp.bfloat16
    )


def solution(mesh):
    in_specs = (P("seq", "head"), P("seq", "head"), P("seq", "head"), P())
    out_specs = P(("seq", "head"), None)
    return jax.shard_map(shards, mesh=mesh, in_specs=in_specs, out_specs=out_specs, check_vma=False)
```

profile of v0, /device:TPU:1, one launch (start us, length us, event | category | flops | bytes accessed | tf_op | source)
XLA Modules:
  0.0 354.0 jit_solution(11749175016474953703)
XLA Ops:
  9.6 4.5 %collective-permute-start.2 = (bf16[2,128,128]{2,0,1:T(2,128)(2,1)S(1)}, bf16[2,128,128]{2,0,1:T(2,128)(2,1)S(1)}, u32[]{:S(2)}, u32[]{:S(2)}) collective-permute-start(bf16[2,128,128]{2,0,1:T(2,128)(2,1)S(1)} %fusion.76), channel_id=1, source_target_pairs={{0,4},{4,8},{8,12},{12,16},{16,20},{20,24},{24,28},{28,32},{32,36}... | collective-permute-start | bytes 196616 | tf_op jit(solution)/shard_map/ppermute | solution.py:20
  14.2 5.6 %collective-permute-start.3 = (bf16[2,128,128]{2,0,1:T(2,128)(2,1)S(1)}, bf16[2,128,128]{2,0,1:T(2,128)(2,1)S(1)}, u32[]{:S(2)}, u32[]{:S(2)}) collective-permute-start(bf16[2,128,128]{2,0,1:T(2,128)(2,1)S(1)} %fusion.76), channel_id=1, source_target_pairs={{4,0},{8,4},{12,8},{16,12},{20,16},{24,20},{28,24},{32,28},{36,32}... | collective-permute-start | bytes 196616 | tf_op jit(solution)/shard_map/ppermute | solution.py:22
  21.9 1.9 collective-permute-start
  23.8 2.4 collective-permute-start.1
  36.7 126.5 %all-gather.3.cloned.1.call-done = bf16[2,16384,1,128]{3,0,2,1:T(2,128)(2,1)} async-done(((bf16[2,128,1,128]{3,0,2,1:T(2,128)(2,1)}), bf16[2,16384,1,128]{3,0,2,1:T(2,128)(2,1)}) %all-gather.3.cloned.1.call-update) | async-done | bytes 8388624 | tf_op jit(solution)/shard_map/all_gather | solution.py:81
  163.2 5.1 %copy.50 = bf16[2,16384,1,128]{3,1,0,2:T(8,128)(2,1)S(1)} copy(bf16[2,16384,1,128]{3,0,2,1:T(2,128)(2,1)} %all-gather.3.cloned.1.call-done) | data formatting | bytes 16777216 | tf_op jit(solution)/shard_map/all_gather | solution.py:81
  168.3 13.0 %fusion.63 = (f32[2,8192,1,128]{3,2,1,0:T(1,128)}, f32[2,8192,1,128]{3,2,1,0:T(1,128)}) fusion(bf16[2,8192,2,128]{3,2,1,0:T(2,128)(2,1)S(1)} %bitcast.97), kind=kLoop, calls=%fused_computation.146 | loop fusion | bytes 33554432 | tf_op jit(solution)/shard_map/slice | solution.py:39
  181.3 18.0 %copy.76 = f32[2,8192,1,128]{1,3,0,2:T(8,128)} copy(f32[2,8192,1,128]{3,2,1,0:T(1,128)} %get-tuple-element.22) | data formatting | bytes 16777216
  199.2 18.0 %copy.77 = f32[2,8192,1,128]{1,3,0,2:T(8,128)} copy(f32[2,8192,1,128]{3,2,1,0:T(1,128)} %get-tuple-element.21) | data formatting | bytes 16777216
  217.2 9.4 %multiply_convert_fusion = bf16[2,8192,1,128]{1,3,0,2:T(8,128)(2,1)} fusion(f32[2,8192,1,128]{1,3,0,2:T(8,128)} %copy.76, f32[2,8192,1,128]{1,3,0,2:T(8,128)} %copy.77), kind=kLoop, calls=%fused_computation.3 | loop fusion | flops 6291456 | bytes 20971520 | tf_op jit(solution)/shard_map/convert_element_type | solution.py:39
  226.7 7.0 %copy.53 = f32[2,8192,1,128]{3,1,0,2:T(8,128)} copy(bf16[2,8192,1,128]{1,3,0,2:T(8,128)(2,1)} %multiply_convert_fusion) | data formatting | bytes 12582912 | tf_op jit(solution)/shard_map/convert_element_type | solution.py:38
  233.7 11.5 %fusion.62 = (f32[2,4096,1,128]{3,2,1,0:T(1,128)}, f32[2,4096,1,128]{3,2,1,0:T(1,128)}) fusion(f32[2,4096,2,128]{3,2,1,0:T(2,128)} %bitcast.102), kind=kLoop, calls=%fused_computation.145 | loop fusion | bytes 16777216 | tf_op jit(solution)/shard_map/slice | solution.py:39
  245.2 10.2 %copy.78 = f32[2,4096,1,128]{1,3,0,2:T(8,128)} copy(f32[2,4096,1,128]{3,2,1,0:T(1,128)} %get-tuple-element.20) | data formatting | bytes 8388608
  255.4 10.2 %copy.79 = f32[2,4096,1,128]{1,3,0,2:T(8,128)} copy(f32[2,4096,1,128]{3,2,1,0:T(1,128)} %get-tuple-element.19) | data formatting | bytes 8388608
  265.6 4.3 %multiply_convert_fusion.1 = bf16[2,4096,1,128]{1,3,0,2:T(8,128)(2,1)S(1)} fusion(f32[2,4096,1,128]{1,3,0,2:T(8,128)} %copy.78, f32[2,4096,1,128]{1,3,0,2:T(8,128)} %copy.79), kind=kLoop, calls=%fused_computation.4 | loop fusion | flops 3145728 | bytes 10485760 | tf_op jit(solution)/shard_map/convert_element_type | solution.py:39
  269.9 2.9 copy.56
  272.8 7.9 %fusion.64 = (f32[2,2048,1,128]{3,2,1,0:T(1,128)}, f32[2,2048,1,128]{3,2,1,0:T(1,128)}) fusion(f32[2,2048,2,128]{3,2,1,0:T(2,128)} %bitcast.105), kind=kLoop, calls=%fused_computation.147 | loop fusion | bytes 8388608 | tf_op jit(solution)/shard_map/slice | solution.py:39
  280.7 6.1 %copy.80 = f32[2,2048,1,128]{1,3,0,2:T(8,128)} copy(f32[2,2048,1,128]{3,2,1,0:T(1,128)} %get-tuple-element.32) | data formatting | bytes 4194304
  286.8 6.1 %copy.81 = f32[2,2048,1,128]{1,3,0,2:T(8,128)} copy(f32[2,2048,1,128]{3,2,1,0:T(1,128)} %get-tuple-element.23) | data formatting | bytes 4194304
  292.9 3.6 %multiply_convert_fusion.2 = bf16[2,2048,1,128]{1,3,0,2:T(8,128)(2,1)} fusion(f32[2,2048,1,128]{1,3,0,2:T(8,128)} %copy.80, f32[2,2048,1,128]{1,3,0,2:T(8,128)} %copy.81), kind=kLoop, calls=%fused_computation.11 | loop fusion | flops 1572864 | bytes 5242880 | tf_op jit(solution)/shard_map/convert_element_type | solution.py:39
  296.5 2.6 copy.59
  299.1 5.4 %fusion.65 = (f32[2,1024,1,128]{3,2,1,0:T(1,128)}, f32[2,1024,1,128]{3,2,1,0:T(1,128)}) fusion(f32[2,1024,2,128]{3,2,1,0:T(2,128)} %bitcast.108), kind=kLoop, calls=%fused_computation.148 | loop fusion | bytes 4194304 | tf_op jit(solution)/shard_map/slice | solution.py:39
  304.6 3.6 %copy.82 = f32[2,1024,1,128]{1,3,0,2:T(8,128)} copy(f32[2,1024,1,128]{3,2,1,0:T(1,128)} %get-tuple-element.36) | data formatting | bytes 2097152
  308.2 3.6 %copy.83 = f32[2,1024,1,128]{1,3,0,2:T(8,128)} copy(f32[2,1024,1,128]{3,2,1,0:T(1,128)} %get-tuple-element.34) | data formatting | bytes 2097152
  314.7 3.5 fusion.66
  318.2 1.9 copy.84
  320.1 1.9 copy.85
  324.3 2.5 fusion.67
  326.8 1.8 copy.86
  328.6 1.8 copy.87
  330.4 2.2 copy-done.1
  338.0 8.3 %all_to_all.19 = bf16[4,64,128]{2,1,0:T(8,128)(2,1)S(1)} all-to-all(bf16[4,64,128]{2,1,0:T(8,128)(2,1)S(1)} %bitcast.121), channel_id=1, replica_groups=mesh['seq'=128,'head'=4] {'head'}, dimensions={0} | all-to-all | bytes 131072 | tf_op jit(solution)/shard_map/all_to_all | solution.py:156
  (117 shorter events, 26.7 us)
Async XLA Ops:
  6.5 339.8 %copy-start = (bf16[512,512]{1,0:T(8,128)(2,1)S(1)}, bf16[512,512]{1,0:T(8,128)(2,1)}, u32[]{:S(2)}) copy-start(bf16[512,512]{1,0:T(8,128)(2,1)} %param.7) | copy-start | bytes 1572868
  6.5 156.7 %all-gather.3.cloned.1.call-start = ((), (), s32[]{:S(2)}) async-start(), calls=%async_computation.1 | async-start | bytes 8454144 | tf_op jit(solution)/shard_map/all_gather | solution.py:81
  9.6 20.1 %collective-permute-start.2 = (bf16[2,128,128]{2,0,1:T(2,128)(2,1)S(1)}, bf16[2,128,128]{2,0,1:T(2,128)(2,1)S(1)}, u32[]{:S(2)}, u32[]{:S(2)}) collective-permute-start(bf16[2,128,128]{2,0,1:T(2,128)(2,1)S(1)} %fusion.76), channel_id=1, source_target_pairs={{0,4},{4,8},{8,12},{12,16},{16,20},{20,24},{24,28},{28,32},{32,36}... | collective-permute-start | bytes 196616 | tf_op jit(solution)/shard_map/ppermute | solution.py:20
  14.2 15.6 %collective-permute-start.3 = (bf16[2,128,128]{2,0,1:T(2,128)(2,1)S(1)}, bf16[2,128,128]{2,0,1:T(2,128)(2,1)S(1)}, u32[]{:S(2)}, u32[]{:S(2)}) collective-permute-start(bf16[2,128,128]{2,0,1:T(2,128)(2,1)S(1)} %fusion.76), channel_id=1, source_target_pairs={{4,0},{8,4},{12,8},{16,12},{20,16},{24,20},{28,24},{32,28},{36,32}... | collective-permute-start | bytes 196616 | tf_op jit(solution)/shard_map/ppermute | solution.py:22
  21.9 10.1 %collective-permute-start = (bf16[2,128,128]{2,0,1:T(2,128)(2,1)S(1)}, bf16[2,128,128]{2,0,1:T(2,128)(2,1)S(1)}, u32[]{:S(2)}, u32[]{:S(2)}) collective-permute-start(bf16[2,128,128]{2,0,1:T(2,128)(2,1)S(1)} %get-tuple-element.45), channel_id=1, source_target_pairs={{0,4},{4,8},{8,12},{12,16},{16,20},{20,24},{24,28},{28,32},{32,36}... | collective-permute-start | bytes 196616 | tf_op jit(solution)/shard_map/ppermute | solution.py:20
  23.8 8.2 %collective-permute-start.1 = (bf16[2,128,128]{2,0,1:T(2,128)(2,1)S(1)}, bf16[2,128,128]{2,0,1:T(2,128)(2,1)S(1)}, u32[]{:S(2)}, u32[]{:S(2)}) collective-permute-start(bf16[2,128,128]{2,0,1:T(2,128)(2,1)S(1)} %get-tuple-element.46), channel_id=1, source_target_pairs={{4,0},{8,4},{12,8},{16,12},{20,16},{24,20},{28,24},{32,28},{36,32}... | collective-permute-start | bytes 196616 | tf_op jit(solution)/shard_map/ppermute | solution.py:22
  31.0 3.3 copy-start.9
  34.3 1.2 copy-start.5
  330.4 2.2 copy-start.1
  332.6 1.2 copy-start.2
  332.7 1.4 copy-start.7
  332.7 1.4 copy-start.8
  333.9 1.1 copy-start.4
  334.0 1.2 copy-start.6
  334.7 1.3 copy-start.3
Sparse Core Ops, SparseCore 0:
  10.5 152.6 all-gather.2
where the time goes:
time: 357 us; the launch traced here: 354 us
  local copies, waits for them, and re-layouts  161 us (45%)
  waiting for transfers between devices  126 us (35%)
  other arithmetic  24 us (7%)
  starting transfers between devices  14.4 us (4%)
  between operations  14 us (4%)
  blocking collectives  8.28 us (2%)
  matrix products  5.36 us (2%)
    all_gather x1, waiting for transfers between devices, shards(): everything = lax.all_gather(own_block, 'seq', axis=1, tiled=True)  126 us
    unnamed x54, local copies, waits for them, and re-layouts  89.9 us
    slice x6, local copies, waits for them, and re-layouts, average_pairs(): return (0.5 * (widened[:, :, 0] + widened[:, :, 1])).astype(jnp.bfloat16)  43.9 us
    convert_element_type x8, other arithmetic, average_pairs(): return (0.5 * (widened[:, :, 0] + widened[:, :, 1])).astype(jnp.bfloat16)  21.3 us
    convert_element_type x5, local copies, waits for them, and re-layouts, average_pairs(): stacked.astype(jnp.float32)  14.7 us
    all_to_all x1, blocking collectives, shards(): lax.all_to_all(as_sent(attended), 'head', split_axis=0, concat_axis=1, ti...  8.28 us
    ppermute x2, starting transfers between devices, extended_2(): lax.ppermute(head, axis, [((i + 1) % count, i) for i in range(ends)])  7.98 us
  transfers between devices with their start and end apart: 5, of which 1 were waited for; matrix products, arithmetic and copies ran while one was open for 4% of the time, Pallas kernels for 0%

commit v1 on v0

v1 whole, which is shorter than its diff:
```python
import math

import jax
import jax.numpy as jnp
from jax import lax
from jax.experimental import pallas as pl
from jax.experimental.pallas import tpu as pltpu
from jax.sharding import PartitionSpec as P

MESH = pl.DeviceIdType.MESH
HD = 64
LEAF = 128
SPAN = 256
PLANE = 8
PLANES = 16
SEQ = PLANE * PLANES
HEADS_DEV = 4
NEAR, FAR = 1152, 512
COLS = NEAR + FAR
ROWS = 4 * LEAF
STRIP = 32
Z, N0, N1, L2, L3, L4, PL, AT, GROUPS = range(9)


def dot_t(a, b):
    return lax.dot_general(a, b, (((1,), (1,)), ((), ())), preferred_element_type=jnp.float32)


def dot(a, b):
    return jnp.dot(a, b, preferred_element_type=jnp.float32)


def pair_mean(rows):
    out = lax.broadcasted_iota(jnp.int32, (rows, 2 * rows), 0)
    inp = lax.broadcasted_iota(jnp.int32, (rows, 2 * rows), 1)
    return jnp.where((inp >> 1) == out, 0.5, 0.0).astype(jnp.bfloat16)


def group_mean(rows):
    out = lax.broadcasted_iota(jnp.int32, (rows, 2 * rows), 0)
    inp = lax.broadcasted_iota(jnp.int32, (rows, 2 * rows), 1)
    group = 2 * (out >> 4) + ((out >> 2) & 1)
    first = group * 16 + (out & 8) + 2 * (out & 3)
    return jnp.where((inp & ~1) == first, 0.5, 0.0).astype(jnp.bfloat16)


def open_if(valid):
    return jnp.where(valid, 0.0, -jnp.inf).astype(jnp.float32)


def bias_row(parts):
    total = sum(width for width, _ in parts)
    col = lax.broadcasted_iota(jnp.int32, (1, total), 1)
    row = jnp.zeros((1, total), jnp.float32)
    low = 0
    for width, value in parts:
        row = jnp.where((col >= low) & (col < low + width), value, row)
        low += width
    return row


def kernel(
    q_hbm, k_hbm, v_hbm, w_hbm, out_ref,
    q, kv, w, s1, s2, s3, s4, n0, n1, r2, r3, r4, zbuf, f5, f6, f7, pbuf,
    qm, scores, probs, total, att, gath,
    local_sem, send_sem, recv_sem,
):
    seq = lax.axis_index("seq")
    head = lax.axis_index("head")
    z = seq // PLANE
    r = seq % PLANE

    loads = [
        pltpu.make_async_copy(k_hbm, kv.at[0], local_sem.at[0]),
        pltpu.make_async_copy(v_hbm, kv.at[1], local_sem.at[1]),
        pltpu.make_async_copy(q_hbm, q, local_sem.at[2]),
        pltpu.make_async_copy(w_hbm, w, local_sem.at[3]),
    ]
    for load in loads:
        load.start()

    prev, following = (seq + SEQ - 1) % SEQ, (seq + 1) % SEQ

    def groups(size):
        index = seq // size
        odd = index % 2
        deltas = [-2, 2, 3 - 6 * odd]
        count = SEQ // size
        valid = [(index + d >= 0) & (index + d < count) for d in deltas]
        return [(index + d + count) % count for d in deltas], valid

    def members(size):
        pos = seq % size
        return [g * size + (pos ^ e) for g in groups(size)[0] for e in range(size)]

    planes = [((z + d) % PLANES) * PLANE + r for d in range(1, PLANES)]
    plane = [z * PLANE + (r ^ e) for e in range(1, PLANE)]
    two, three, four = members(1), members(2), members(4)
    heads = [head ^ e for e in range(1, HEADS_DEV)]

    barrier = pltpu.get_barrier_semaphore()
    met = [prev, following, *planes, *plane, *two, *three, *four]
    for t in met:
        pl.semaphore_signal(barrier, inc=1, device_id={"seq": t}, device_id_type=MESH)
    for t in heads:
        pl.semaphore_signal(barrier, inc=1, device_id={"head": t}, device_id_type=MESH)

    def send(src, dst, group, to):
        pltpu.make_async_remote_copy(
            src_ref=src, dst_ref=dst, send_sem=send_sem.at[group], recv_sem=recv_sem.at[group],
            device_id=to, device_id_type=MESH,
        ).start()

    def arrived(ref, group):
        pltpu.make_async_copy(ref, ref, recv_sem.at[group]).wait()

    def sent(ref, group):
        pltpu.make_async_copy(ref, ref, send_sem.at[group]).wait()

    loads[0].wait()
    loads[1].wait()
    both = jnp.concatenate([kv[0], kv[1]], axis=1)
    mean = pair_mean(LEAF)
    level = both
    for dst, rows in ((s1, 128), (s2, 64), (s3, 32), (s4, 16)):
        level = dot(mean[:rows, : 2 * rows], level).astype(jnp.bfloat16)
        dst[0] = level[:, :128]
        dst[1] = level[:, 128:]
    last = dot(mean[:8, :16], level)
    zbuf[z] = jnp.concatenate([last[:, :128], last[:, 128:]], axis=0).astype(jnp.bfloat16)

    pl.semaphore_wait(barrier, len(met) + len(heads))
    for t in planes:
        send(zbuf.at[z], zbuf.at[z], Z, {"seq": t})
    send(kv.at[:, pl.ds(LEAF, LEAF)], n0.at[0], N0, {"seq": following})
    send(kv.at[:, pl.ds(0, LEAF)], n0.at[1], N0, {"seq": prev})
    send(s1, n1.at[0], N1, {"seq": following})
    send(s1, n1.at[1], N1, {"seq": prev})
    def scatter(src, dst, group, targets):
        size = len(targets) // 3
        for i, t in enumerate(targets):
            slot = ((1, 0, 2)[i // size]) * size + i % size
            send(src, dst.at[slot], group, {"seq": t})

    scatter(s2, r2, L2, two)
    scatter(s3, r3, L3, three)
    scatter(s4, r4, L4, four)

    loads[2].wait()
    lane = lax.broadcasted_iota(jnp.int32, (LEAF, LEAF), 1)
    for leaf in range(2):
        block = q[leaf * LEAF : (leaf + 1) * LEAF] * jnp.bfloat16(1.0 / math.sqrt(HD))
        qm[leaf, :LEAF] = jnp.where(lane < HD, block, jnp.bfloat16(0))
        qm[leaf, LEAF:] = jnp.where(lane < HD, jnp.bfloat16(0), block)

    def put(leaf, low, keys, bias=None):
        part = dot_t(qm[leaf], keys)
        if bias is not None:
            part = part + bias
        scores[leaf * SPAN : (leaf + 1) * SPAN, low : low + keys.shape[0]] = part

    put(0, LEAF, kv[0])
    put(1, 0, kv[0])

    arrived(zbuf.at[pl.ds(0, PLANES - 1)], Z)
    fifth = zbuf[...].reshape(PLANES * 16, LEAF)
    f5[...] = fifth.astype(jnp.float32)
    mean = group_mean(LEAF)
    sixth = dot(mean, fifth).astype(jnp.bfloat16)
    f6[...] = sixth.astype(jnp.float32)
    f7[...] = dot(mean[:64, :128], sixth).astype(jnp.bfloat16).astype(jnp.float32)
    fifths, valid5 = groups(PLANE)
    sixths, valid6 = groups(2 * PLANE)
    seventh = z // 4
    step = 3 - 6 * (seventh % 2)
    sevenths = [(seventh + 2) % 4, (seventh + step + 4) % 4]
    valid7 = [None, (seventh + step >= 0) & (seventh + step < 4)]
    picks = [(f5, g) for g in fifths] + [(f6, g) for g in sixths] + [(f7, g) for g in sevenths]
    for side in range(2):
        rows = [ref[pl.ds(pl.multiple_of(g * 16 + side * 8, 8), 8), :] for ref, g in picks]
        pbuf[0, side] = jnp.concatenate(rows, axis=0).astype(jnp.bfloat16)
    for e, t in enumerate(plane):
        send(pbuf.at[0], pbuf.at[e + 1], PL, {"seq": t})

    has_prev, has_next = open_if(seq >= 1), open_if(seq + 1 < SEQ)
    bias2 = [(64, open_if(ok)) for ok in groups(1)[1]]
    bias34 = [(64, open_if(ok)) for size in (2, 4) for ok in groups(size)[1]]
    arrived(n0, N0)
    put(0, 0, n0[0, 0], has_prev)
    put(1, SPAN, n0[1, 0], has_next)
    arrived(n1, N1)
    arrived(r2, L2)
    second = r2[:, 0].reshape(192, LEAF)
    low_keys = jnp.concatenate([n1[0, 0, :64], n1[1, 0], second], axis=0)
    put(0, 384, low_keys, bias_row([(64, has_prev), (128, has_next), *bias2]))
    high_keys = jnp.concatenate([n1[0, 0], n1[1, 0, 64:], second], axis=0)
    put(1, 384, high_keys, bias_row([(128, has_prev), (64, has_next), *bias2]))
    arrived(r3, L3)
    arrived(r4, L4)
    keys = jnp.concatenate([r3[:, 0].reshape(192, LEAF), r4[:, 0].reshape(192, LEAF)], axis=0)
    row = bias_row(bias34)
    put(0, 768, keys, row)
    put(1, 768, keys, row)

    arrived(pbuf.at[pl.ds(0, PLANE - 1)], PL)
    col = lax.broadcasted_iota(jnp.int32, (1, FAR), 1)
    which = (col >> 3) & 7
    row = jnp.zeros((1, FAR), jnp.float32)
    for i, ok in enumerate([*valid5, *valid6, *valid7]):
        if ok is not None:
            row = jnp.where(which == i, open_if(ok), row)
    keys = pbuf[:, 0].reshape(FAR, LEAF)
    put(0, NEAR, keys, row)
    put(1, NEAR, keys, row)

    for low in range(0, ROWS, STRIP):
        strip = scores[low : low + STRIP]
        weights = jnp.exp(strip - jnp.max(strip, axis=1, keepdims=True))
        total[low : low + STRIP] = jnp.sum(weights, axis=1, keepdims=True)
        probs[low : low + STRIP] = weights.astype(jnp.bfloat16)

    second = r2[:, 1].reshape(192, LEAF)
    middle = jnp.concatenate([r3[:, 1].reshape(192, LEAF), r4[:, 1].reshape(192, LEAF)], axis=0)
    far = pbuf[:, 1].reshape(FAR, LEAF)
    near = (
        (n0[0, 1], kv[1], n1[0, 1, :64], n1[1, 1], second, middle, far),
        (kv[1], n0[1, 1], n1[0, 1], n1[1, 1, 64:], second, middle, far),
    )
    for leaf in range(2):
        rows = slice(leaf * SPAN, (leaf + 1) * SPAN)
        numer = dot(probs[rows], jnp.concatenate(near[leaf], axis=0))
        numer = numer / total[rows]
        rows_out = jnp.where(lane < HD, numer[:LEAF], numer[LEAF:]).astype(jnp.bfloat16)
        att[2 * leaf] = rows_out[:64]
        att[2 * leaf + 1] = rows_out[64:]

    gath[head] = att[head]
    for t in heads:
        send(att.at[t], gath.at[head], AT, {"head": t})
    loads[3].wait()
    arrived(gath.at[pl.ds(0, HEADS_DEV - 1)], AT)
    rows = jnp.concatenate([gath[i] for i in range(HEADS_DEV)], axis=1)
    out_ref[...] = dot(rows, w[...]).astype(jnp.bfloat16)

    sent(zbuf.at[pl.ds(0, PLANES - 1)], Z)
    sent(n0, N0)
    sent(n1, N1)
    sent(r2, L2)
    sent(r3, L3)
    sent(r4, L4)
    sent(pbuf.at[pl.ds(0, PLANE - 1)], PL)
    sent(gath.at[pl.ds(0, HEADS_DEV - 1)], AT)


def shards(queries, keys, values, out_weight):
    bf16, f32 = jnp.bfloat16, jnp.float32
    any_space = pl.BlockSpec(memory_space=pl.ANY)
    scratch = [
        ((SPAN, LEAF), bf16),
        ((2, SPAN, LEAF), bf16),
        ((512, 512), bf16),
        ((2, 128, LEAF), bf16),
        ((2, 64, LEAF), bf16),
        ((2, 32, LEAF), bf16),
        ((2, 16, LEAF), bf16),
        ((2, 2, LEAF, LEAF), bf16),
        ((2, 2, LEAF, LEAF), bf16),
        ((3, 2, 64, LEAF), bf16),
        ((6, 2, 32, LEAF), bf16),
        ((12, 2, 16, LEAF), bf16),
        ((PLANES, 16, LEAF), bf16),
        ((256, LEAF), f32),
        ((128, LEAF), f32),
        ((64, LEAF), f32),
        ((PLANE, 2, 64, LEAF), bf16),
        ((2, SPAN, LEAF), bf16),
        ((ROWS, COLS), f32),
        ((ROWS, COLS), bf16),
        ((ROWS, 1), f32),
        ((HEADS_DEV, 64, LEAF), bf16),
        ((HEADS_DEV, 64, LEAF), bf16),
    ]
    return pl.pallas_call(
        kernel,
        out_shape=jax.ShapeDtypeStruct((64, 512), bf16),
        in_specs=[any_space] * 4,
        out_specs=pl.BlockSpec(memory_space=pltpu.VMEM),
        scratch_shapes=[
            *(pltpu.VMEM(shape, kind) for shape, kind in scratch),
            pltpu.SemaphoreType.DMA((4,)),
            pltpu.SemaphoreType.DMA((GROUPS,)),
            pltpu.SemaphoreType.DMA((GROUPS,)),
        ],
        compiler_params=pltpu.CompilerParams(
            collective_id=0, has_side_effects=True, vmem_limit_bytes=40 * 2**20
        ),
    )(queries, keys, values, out_weight)


def solution(mesh):
    in_specs = (P("seq", "head"), P("seq", "head"), P("seq", "head"), P())
    out_specs = P(("seq", "head"), None)
    return jax.shard_map(shards, mesh=mesh, in_specs=in_specs, out_specs=out_specs, check_vma=False)
```

time: 357 us -> 38.7 us (0.11)
  local copies, waits for them, and re-layouts: 161 us -> 4.19 us
  waiting for transfers between devices: 126 us -> 0 us
  Pallas kernels: 0 us -> 34.2 us
  other arithmetic: 24 us -> 0 us
  starting transfers between devices: 14.4 us -> 0 us
  between operations: 14 us -> 0.01 us
  blocking collectives: 8.28 us -> 0 us
  matrix products: 5.36 us -> 0 us
    all_gather x1 -> x0, waiting for transfers between devices: 126 us -> none  [shards(): everything = lax.all_gather(own_block, 'seq', axis=1, tiled=True)]
    unnamed x54 -> x9, local copies, waits for them, and re-layouts: 89.9 us -> 4.19 us
    slice x6 -> x0, local copies, waits for them, and re-layouts: 43.9 us -> none  [average_pairs(): return (0.5 * (widened[:, :, 0] + widened[:, :, 1])).astype(jnp.bfloat16)]
    pallas_call x0 -> x1, Pallas kernels: none -> 34.2 us  [shards(): pl.pallas_call(kernel, out_shape=jax.ShapeDtypeStruct((64, 512), bf16), i...]
    convert_element_type x9 -> x0, other arithmetic: 21.6 us -> none  [the longest x8 21.3 us: average_pairs(): return (0.5 * (widened[:, :, 0] + widened[:, :, 1])).astype(jnp.bfloat16)]
    convert_element_type x5 -> x0, local copies, waits for them, and re-layouts: 14.7 us -> none  [average_pairs(): stacked.astype(jnp.float32)]
    ppermute x4 -> x0, starting transfers between devices: 14.4 us -> none  [the longest x2 7.98 us: extended_2(): lax.ppermute(head, axis, [((i + 1) % count, i) for i in range(ends)])]
    all_to_all x1 -> x0, blocking collectives: 8.28 us -> none  [shards(): lax.all_to_all(as_sent(attended), 'head', split_axis=0, concat_axis=1, ti...]
  transfers between devices with their start and end apart: 5 -> 0, of which waited for: 1 -> 0; matrix products, arithmetic and copies ran while one was open for 4% -> 0% of each run, Pallas kernels for 0% -> 0%
where the time goes in v1:
time: 38.7 us; the launch traced here: 38.4 us
  Pallas kernels  34.2 us (88%)
  local copies, waits for them, and re-layouts  4.19 us (11%)
    pallas_call x1, Pallas kernels, shards(): pl.pallas_call(kernel, out_shape=jax.ShapeDtypeStruct((64, 512), bf16), i...  34.2 us
    unnamed x9, local copies, waits for them, and re-layouts  4.19 us

profile of v1, /device:TPU:1, one launch (start us, length us, event | category | flops | bytes accessed | tf_op | source)
XLA Modules:
  0.0 38.4 jit_solution(6383627130687232675)
XLA Ops:
  0.0 0.0 copy-start
  0.0 1.0 %copy-done = bf16[512,512]{1,0:T(8,128)(2,1)S(1)} copy-done((bf16[512,512]{1,0:T(8,128)(2,1)S(1)}, bf16[512,512]{1,0:T(8,128)(2,1)}, u32[]{:S(2)}) %copy-start) | copy-done | bytes 524312
  1.0 0.0 copy-start.1
  1.0 0.8 %copy-done.1 = bf16[256,128]{1,0:T(8,128)(2,1)S(1)} copy-done((bf16[256,128]{1,0:T(8,128)(2,1)S(1)}, bf16[256,128]{1,0:T(8,128)(2,1)}, u32[]{:S(2)}) %copy-start.1) | copy-done | bytes 65560
  1.9 0.0 copy-start.2
  1.9 0.8 %copy-done.2 = bf16[256,128]{1,0:T(8,128)(2,1)S(1)} copy-done((bf16[256,128]{1,0:T(8,128)(2,1)S(1)}, bf16[256,128]{1,0:T(8,128)(2,1)}, u32[]{:S(2)}) %copy-start.2) | copy-done | bytes 65560
  2.7 0.0 copy-start.3
  2.7 0.8 %copy-done.3 = bf16[256,128]{1,0:T(8,128)(2,1)S(1)} copy-done((bf16[256,128]{1,0:T(8,128)(2,1)S(1)}, bf16[256,128]{1,0:T(8,128)(2,1)}, u32[]{:S(2)}) %copy-start.3) | copy-done | bytes 65560
  3.6 34.2 %shard_map.46 = bf16[64,512]{1,0:T(8,128)(2,1)S(1)} custom-call(bf16[256,128]{1,0:T(8,128)(2,1)S(1)} %copy-done.1, bf16[256,128]{1,0:T(8,128)(2,1)S(1)} %copy-done.2, bf16[256,128]{1,0:T(8,128)(2,1)S(1)} %copy-done.3, bf16[512,512]{1,0:T(8,128)(2,1)S(1)} %copy-done), custom_call_target="tpu_custom_call" | custom-call | tf_op jit(solution)/shard_map/pallas_call | solution.py:283
  37.8 0.6 %copy.6 = bf16[64,512]{1,0:T(8,128)(2,1)} copy(bf16[64,512]{1,0:T(8,128)(2,1)S(1)} %shard_map.46) | data formatting | bytes 131072
Async XLA Ops:
  0.0 1.0 %copy-start = (bf16[512,512]{1,0:T(8,128)(2,1)S(1)}, bf16[512,512]{1,0:T(8,128)(2,1)}, u32[]{:S(2)}) copy-start(bf16[512,512]{1,0:T(8,128)(2,1)} %w_hbm.1) | copy-start | bytes 1572868
  1.0 0.8 %copy-start.1 = (bf16[256,128]{1,0:T(8,128)(2,1)S(1)}, bf16[256,128]{1,0:T(8,128)(2,1)}, u32[]{:S(2)}) copy-start(bf16[256,128]{1,0:T(8,128)(2,1)} %q_hbm.1) | copy-start | bytes 196612
  1.9 0.8 %copy-start.2 = (bf16[256,128]{1,0:T(8,128)(2,1)S(1)}, bf16[256,128]{1,0:T(8,128)(2,1)}, u32[]{:S(2)}) copy-start(bf16[256,128]{1,0:T(8,128)(2,1)} %k_hbm.1) | copy-start | bytes 196612
  2.7 0.8 %copy-start.3 = (bf16[256,128]{1,0:T(8,128)(2,1)S(1)}, bf16[256,128]{1,0:T(8,128)(2,1)}, u32[]{:S(2)}) copy-start(bf16[256,128]{1,0:T(8,128)(2,1)} %v_hbm.1) | copy-start | bytes 196612

commit v2 on v1

v2 whole, which is shorter than its diff:
```python
import math

import jax
import jax.numpy as jnp
from jax import lax
from jax.experimental import pallas as pl
from jax.experimental.pallas import tpu as pltpu
from jax.sharding import PartitionSpec as P

MESH = pl.DeviceIdType.MESH
HD = 64
LEAF = 128
SPAN = 256
PLANE = 8
PLANES = 16
SEQ = PLANE * PLANES
HEADS_DEV = 4
NEAR, MID, FAR = 1152, 384, 128
COLS = NEAR + MID + FAR
EARLY = 4
ROWS = 4 * LEAF
STRIP = 32
N0, N1, L2, L3, L4, PM, PF, AT, Z5, Z6, Z7, GROUPS = 0, 2, 4, 7, 10, 13, 14, 15, 16, 19, 22, 24


def dot_t(a, b):
    return lax.dot_general(a, b, (((1,), (1,)), ((), ())), preferred_element_type=jnp.float32)


def dot(a, b):
    return jnp.dot(a, b, preferred_element_type=jnp.float32)


def pair_mean(rows):
    out = lax.broadcasted_iota(jnp.int32, (rows, 2 * rows), 0)
    inp = lax.broadcasted_iota(jnp.int32, (rows, 2 * rows), 1)
    return jnp.where((inp >> 1) == out, 0.5, 0.0).astype(jnp.bfloat16)


def group_mean(rows):
    out = lax.broadcasted_iota(jnp.int32, (rows, 2 * rows), 0)
    inp = lax.broadcasted_iota(jnp.int32, (rows, 2 * rows), 1)
    group = 2 * (out >> 4) + ((out >> 2) & 1)
    first = group * 16 + (out & 8) + 2 * (out & 3)
    return jnp.where((inp & ~1) == first, 0.5, 0.0).astype(jnp.bfloat16)


def open_if(valid):
    return jnp.where(valid, 0.0, -jnp.inf).astype(jnp.float32)


def bias_row(parts):
    total = sum(width for width, _ in parts)
    col = lax.broadcasted_iota(jnp.int32, (1, total), 1)
    row = jnp.zeros((1, total), jnp.float32)
    low = 0
    for width, value in parts:
        row = jnp.where((col >= low) & (col < low + width), value, row)
        low += width
    return row


def kernel(
    q_hbm, k_hbm, v_hbm, w_hbm, out_ref,
    q, kv, w, s1, s2, s3, s4, n0, n1, r2, r3, r4, zbuf, pmid, pfar,
    qm, scores, probs, total, att, gath,
    local_sem, send_sem, recv_sem, open_sem,
):
    seq = lax.axis_index("seq")
    head = lax.axis_index("head")
    z = seq // PLANE
    r = seq % PLANE

    loads = [
        pltpu.make_async_copy(k_hbm, kv.at[0], local_sem.at[0]),
        pltpu.make_async_copy(v_hbm, kv.at[1], local_sem.at[1]),
        pltpu.make_async_copy(q_hbm, q, local_sem.at[2]),
        pltpu.make_async_copy(w_hbm, w, local_sem.at[3]),
    ]
    for load in loads:
        load.start()

    def groups(size):
        index = seq // size
        odd = index % 2
        deltas = [-2, 2, 3 - 6 * odd]
        count = SEQ // size
        valid = [(index + d >= 0) & (index + d < count) for d in deltas]
        return [(index + d + count) % count for d in deltas], valid

    plane = [z * PLANE + (r ^ e) for e in (4, 5, 6, 7, 2, 3, 1)]
    heads = [head ^ e for e in (2, 1, 3)]

    zbuf[...] = jnp.zeros_like(zbuf)

    @pl.when((z == 0) | (z == PLANES - 1))
    def _():
        for ref in (n0, n1, r2, r3, r4):
            ref[...] = jnp.zeros_like(ref)

    def tell(sem, **to):
        pl.semaphore_signal(sem, inc=1, device_id=to, device_id_type=MESH)

    barrier = pltpu.get_barrier_semaphore()
    for d in (8, 7, 9, 6, 10, 5, 11, 4, 12, 3, 13, 2, 14, 15):
        pl.when(z + d < PLANES)(lambda d=d: tell(barrier, seq=seq + d * PLANE))
        pl.when((z - d >= 0) & (z - d < EARLY))(lambda d=d: tell(barrier, seq=seq - d * PLANE))
    for t in heads:
        tell(barrier, head=t)
    for t in plane:
        tell(barrier, seq=t)
    for d in (1, -1):

        @pl.when((z + d >= 0) & (z + d < PLANES))
        def _(d=d):
            for e in range(PLANE):
                tell(barrier, seq=(z + d) * PLANE + (r ^ e))

    above = (z + 1 < PLANES).astype(jnp.int32)
    below = (z > 0).astype(jnp.int32)
    partners = len(plane) + len(heads) + PLANE * (above + below)
    partners += jnp.where(z < EARLY, PLANES - 1 - above - below, z - below)

    def send(src, dst, group, to):
        pltpu.make_async_remote_copy(
            src_ref=src, dst_ref=dst, send_sem=send_sem.at[group], recv_sem=recv_sem.at[group],
            device_id=to, device_id_type=MESH,
        ).start()

    def arrived(ref, group):
        pltpu.make_async_copy(ref, ref, recv_sem.at[group]).wait()

    def sent(ref, group):
        pltpu.make_async_copy(ref, ref, send_sem.at[group]).wait()

    loads[0].wait()
    loads[1].wait()
    both = jnp.concatenate([kv[0], kv[1]], axis=1)
    mean = pair_mean(LEAF)
    level = both
    for dst, rows in ((s1, 128), (s2, 64), (s3, 32), (s4, 16)):
        level = dot(mean[:rows, : 2 * rows], level).astype(jnp.bfloat16)
        dst[0] = level[:, :128]
        dst[1] = level[:, 128:]
    last = dot(mean[:8, :16], level)
    zbuf[z] = jnp.concatenate([last[:, :128], last[:, 128:]], axis=0).astype(jnp.bfloat16)

    pl.semaphore_wait(barrier, partners)

    seventh = z // 4
    step = 3 - 6 * (seventh % 2)
    sevenths = [(seventh + 2) % 4, jnp.clip(seventh + step, 0, 3)]
    valid7 = [seventh >= 0, (seventh + step >= 0) & (seventh + step < 4)]
    (sixths, valid6), (fifths, valid5) = groups(2 * PLANE), groups(PLANE)
    classes = (
        (Z7, 4, sevenths, valid7, (0, 1)),
        (Z6, 2, sixths, valid6, (1, 0, 2)),
        (Z5, 1, fifths, valid5, (1, 0, 2)),
    )
    def each_group(ready):
        for group, size, others, valid, slots in classes:
            for i, (other, ok, slot) in enumerate(zip(others, valid, slots, strict=True)):
                targets = [(other * size + (z % size ^ e)) * PLANE + r for e in range(size)]

                def push(targets=targets, group=group, slot=slot):
                    for t in targets:
                        send(zbuf.at[z], zbuf.at[z], group + slot, {"seq": t})

                def admit(targets=targets, group=group, slot=slot):
                    for t in targets:
                        tell(open_sem.at[group - Z5 + slot], seq=t)

                def await_open(group=group, i=i, size=size):
                    pl.semaphore_wait(open_sem.at[group - Z5 + i], size)

                ready(ok, other * size, push, admit, await_open)

    def first_packets(ok, low, push, admit, await_open):
        pl.when(ok & ((low < z) | (z < EARLY)))(push)
        pl.when(ok & (low < z) & (low >= EARLY))(admit)

    def later_packets(ok, low, push, admit, await_open):
        @pl.when(ok & (low > z) & (z >= EARLY))
        def _():
            await_open()
            push()

    each_group(first_packets)

    def packets(wait, which):
        group, size, _, valid, slots = classes[which]
        for i, ok in enumerate(valid):
            slot = slots[i] if wait is sent else i
            pl.when(ok)(lambda slot=slot: wait(zbuf.at[pl.ds(0, size)], group + slot))

    def gathered(which):
        _, size, others, valid, _ = classes[which]
        picks = [jnp.where(ok, other, z // size) for other, ok in zip(others, valid, strict=True)]
        rows = [zbuf[pl.ds(g * size, size)].reshape(size * 16, LEAF) for g in picks]
        return jnp.concatenate(rows, axis=0)

    def forward(rows, dst, group):
        rows = rows.reshape(rows.shape[0] // 16, 2, 8, LEAF)
        for side in range(2):
            half = jnp.concatenate([rows[i, side] for i in range(rows.shape[0])], axis=0)
            dst[0, side] = half.astype(jnp.bfloat16)
        for e, t in enumerate(plane):
            send(dst.at[0], dst.at[e + 1], group, {"seq": t})

    has_prev, has_next = seq >= 1, seq + 1 < SEQ
    chain = ((L2, 1, s2, r2), (L3, 2, s3, r3), (L4, 4, s4, r4))

    @pl.when(has_next)
    def _():
        send(kv.at[:, pl.ds(LEAF, LEAF)], n0.at[0], N0, {"seq": seq + 1})
        send(s1, n1.at[0], N1, {"seq": seq + 1})

    @pl.when(has_prev)
    def _():
        send(kv.at[:, pl.ds(0, LEAF)], n0.at[1], N0 + 1, {"seq": seq - 1})
        send(s1, n1.at[1], N1 + 1, {"seq": seq - 1})

    for group, size, src, dst in chain:
        for i, (other, ok) in enumerate(zip(*groups(size), strict=True)):

            @pl.when(ok)
            def _(group=group, size=size, src=src, dst=dst, i=i, other=other):
                slot = (1, 0, 2)[i]
                for e in range(size):
                    to = other * size + (seq % size ^ e)
                    send(src, dst.at[slot * size + e], group + slot, {"seq": to})

    def near_done(wait, here, slots):
        for group, ref in ((N0, n0), (N1, n1)):
            pl.when(has_prev)(lambda group=group, ref=ref: wait(ref.at[0], group + here))
            pl.when(has_next)(lambda group=group, ref=ref: wait(ref.at[1], group + 1 - here))
        for group, size, _, dst in chain:
            for i, ok in enumerate(groups(size)[1]):
                k = slots[i]
                pl.when(ok)(lambda g=group, n=size, d=dst, k=k: wait(d.at[pl.ds(k * n, n)], g + k))

    loads[2].wait()
    lane = lax.broadcasted_iota(jnp.int32, (LEAF, LEAF), 1)
    for leaf in range(2):
        block = q[leaf * LEAF : (leaf + 1) * LEAF] * jnp.bfloat16(1.0 / math.sqrt(HD))
        qm[leaf, :LEAF] = jnp.where(lane < HD, block, jnp.bfloat16(0))
        qm[leaf, LEAF:] = jnp.where(lane < HD, jnp.bfloat16(0), block)

    def put(leaf, low, keys, bias=None):
        part = dot_t(qm[leaf], keys)
        if bias is not None:
            part = part + bias
        scores[leaf * SPAN : (leaf + 1) * SPAN, low : low + keys.shape[0]] = part

    put(0, LEAF, kv[0])
    put(1, 0, kv[0])

    each_group(later_packets)

    packets(arrived, 2)
    packets(arrived, 1)
    mean = group_mean(64)
    sixth = dot(mean[:48, :96], gathered(1))
    forward(jnp.concatenate([gathered(2).astype(jnp.float32), sixth], axis=0), pmid, PM)

    packets(arrived, 0)
    sixth = dot(mean, gathered(0)).astype(jnp.bfloat16)
    forward(dot(mean[:32, :64], sixth), pfar, PF)

    bias_prev, bias_next = open_if(has_prev), open_if(has_next)
    bias2 = [(64, open_if(ok)) for ok in groups(1)[1]]
    bias34 = [(64, open_if(ok)) for size in (2, 4) for ok in groups(size)[1]]
    near_done(arrived, 0, (0, 1, 2))
    put(0, 0, n0[0, 0], bias_prev)
    put(1, SPAN, n0[1, 0], bias_next)
    second = r2[:, 0].reshape(192, LEAF)
    low_keys = jnp.concatenate([n1[0, 0, :64], n1[1, 0], second], axis=0)
    put(0, 384, low_keys, bias_row([(64, bias_prev), (128, bias_next), *bias2]))
    high_keys = jnp.concatenate([n1[0, 0], n1[1, 0, 64:], second], axis=0)
    put(1, 384, high_keys, bias_row([(128, bias_prev), (64, bias_next), *bias2]))
    keys = jnp.concatenate([r3[:, 0].reshape(192, LEAF), r4[:, 0].reshape(192, LEAF)], axis=0)
    row = bias_row(bias34)
    put(0, 768, keys, row)
    put(1, 768, keys, row)

    biases = [(8, open_if(ok)) for ok in [*valid5, *valid6]]
    row = bias_row(biases * PLANE)
    arrived(pmid.at[pl.ds(0, PLANE - 1)], PM)
    keys = pmid[:, 0].reshape(MID, LEAF)
    put(0, NEAR, keys, row)
    put(1, NEAR, keys, row)
    row = bias_row([(8, open_if(ok)) for ok in valid7] * PLANE)
    arrived(pfar.at[pl.ds(0, PLANE - 1)], PF)
    keys = pfar[:, 0].reshape(FAR, LEAF)
    put(0, NEAR + MID, keys, row)
    put(1, NEAR + MID, keys, row)

    for low in range(0, ROWS, STRIP):
        strip = scores[low : low + STRIP]
        weights = jnp.exp(strip - jnp.max(strip, axis=1, keepdims=True))
        total[low : low + STRIP] = jnp.sum(weights, axis=1, keepdims=True)
        probs[low : low + STRIP] = weights.astype(jnp.bfloat16)

    second = r2[:, 1].reshape(192, LEAF)
    middle = jnp.concatenate([r3[:, 1].reshape(192, LEAF), r4[:, 1].reshape(192, LEAF)], axis=0)
    far = [pmid[:, 1].reshape(MID, LEAF), pfar[:, 1].reshape(FAR, LEAF)]
    near = (
        (n0[0, 1], kv[1], n1[0, 1, :64], n1[1, 1], second, middle, *far),
        (kv[1], n0[1, 1], n1[0, 1], n1[1, 1, 64:], second, middle, *far),
    )
    for leaf in range(2):
        rows = slice(leaf * SPAN, (leaf + 1) * SPAN)
        numer = dot(probs[rows], jnp.concatenate(near[leaf], axis=0))
        numer = numer / total[rows]
        rows_out = jnp.where(lane < HD, numer[:LEAF], numer[LEAF:]).astype(jnp.bfloat16)
        att[2 * leaf] = rows_out[:64]
        att[2 * leaf + 1] = rows_out[64:]

    gath[head] = att[head]
    for t in heads:
        send(att.at[t], gath.at[head], AT, {"head": t})
    loads[3].wait()
    arrived(gath.at[pl.ds(0, HEADS_DEV - 1)], AT)
    rows = jnp.concatenate([gath[i] for i in range(HEADS_DEV)], axis=1)
    out_ref[...] = dot(rows, w[...]).astype(jnp.bfloat16)

    for which in range(3):
        packets(sent, which)
    near_done(sent, 1, (1, 0, 2))
    sent(pmid.at[pl.ds(0, PLANE - 1)], PM)
    sent(pfar.at[pl.ds(0, PLANE - 1)], PF)
    sent(gath.at[pl.ds(0, HEADS_DEV - 1)], AT)


def shards(queries, keys, values, out_weight):
    bf16, f32 = jnp.bfloat16, jnp.float32
    hbm = pl.BlockSpec(memory_space=pltpu.HBM)
    scratch = [
        ((SPAN, LEAF), bf16),
        ((2, SPAN, LEAF), bf16),
        ((512, 512), bf16),
        ((2, 128, LEAF), bf16),
        ((2, 64, LEAF), bf16),
        ((2, 32, LEAF), bf16),
        ((2, 16, LEAF), bf16),
        ((2, 2, LEAF, LEAF), bf16),
        ((2, 2, LEAF, LEAF), bf16),
        ((3, 2, 64, LEAF), bf16),
        ((6, 2, 32, LEAF), bf16),
        ((12, 2, 16, LEAF), bf16),
        ((PLANES, 16, LEAF), bf16),
        ((PLANE, 2, 48, LEAF), bf16),
        ((PLANE, 2, 16, LEAF), bf16),
        ((2, SPAN, LEAF), bf16),
        ((ROWS, COLS), f32),
        ((ROWS, COLS), bf16),
        ((ROWS, 1), f32),
        ((HEADS_DEV, 64, LEAF), bf16),
        ((HEADS_DEV, 64, LEAF), bf16),
    ]
    return pl.pallas_call(
        kernel,
        out_shape=jax.ShapeDtypeStruct((64, 512), bf16),
        in_specs=[hbm] * 4,
        out_specs=pl.BlockSpec(memory_space=pltpu.VMEM),
        scratch_shapes=[
            *(pltpu.VMEM(shape, kind) for shape, kind in scratch),
            pltpu.SemaphoreType.DMA((4,)),
            pltpu.SemaphoreType.DMA((GROUPS,)),
            pltpu.SemaphoreType.DMA((GROUPS,)),
            pltpu.SemaphoreType.REGULAR((GROUPS - Z5,)),
        ],
        compiler_params=pltpu.CompilerParams(
            collective_id=0, has_side_effects=True, vmem_limit_bytes=63_400_000
        ),
    )(queries, keys, values, out_weight)


def solution(mesh):
    in_specs = (P("seq", "head"), P("seq", "head"), P("seq", "head"), P())
    out_specs = P(("seq", "head"), None)
    return jax.shard_map(shards, mesh=mesh, in_specs=in_specs, out_specs=out_specs, check_vma=False)
```

time: 38.7 us -> 35.8 us (0.925)
  the two profiles are of different devices: /device:TPU:1 before, /device:TPU:32 now
where the time goes in v2:
time: 35.8 us; the launch traced here: 35.7 us
  Pallas kernels  34.2 us (96%)
  local copies, waits for them, and re-layouts  1.47 us (4%)
    pallas_call x1, Pallas kernels, shards(): pl.pallas_call(kernel, out_shape=jax.ShapeDtypeStruct((64, 512), bf16), i...  34.2 us
    unnamed x1, local copies, waits for them, and re-layouts  1.47 us

profile of v2, /device:TPU:32, one launch (start us, length us, event | category | flops | bytes accessed | tf_op | source)
XLA Modules:
  0.0 35.7 jit_solution(12185291451924943452)
XLA Ops:
  0.0 34.2 %shard_map.46 = bf16[64,512]{1,0:T(8,128)(2,1)} custom-call(bf16[256,128]{1,0:T(8,128)(2,1)} %q_hbm.1, bf16[256,128]{1,0:T(8,128)(2,1)} %k_hbm.1, bf16[256,128]{1,0:T(8,128)(2,1)} %v_hbm.1, bf16[512,512]{1,0:T(8,128)(2,1)} %w_hbm.1), custom_call_target="tpu_custom_call" | custom-call | tf_op jit(solution)/shard_map/pallas_call | solution.py:361
  34.2 1.5 %copy.6 = bf16[64,512]{1,0:T(8,128)(2,1)} copy(bf16[64,512]{1,0:T(8,128)(2,1)} %shard_map.46) | data formatting | bytes 131072

commit v3 on v2

--- a/solution.py
+++ b/solution.py
@@ -17,7 +17,6 @@
 HEADS_DEV = 4
 NEAR, MID, FAR = 1152, 384, 128
 COLS = NEAR + MID + FAR
-EARLY = 4
 ROWS = 4 * LEAF
 STRIP = 32
 N0, N1, L2, L3, L4, PM, PF, AT, Z5, Z6, Z7, GROUPS = 0, 2, 4, 7, 10, 13, 14, 15, 16, 19, 22, 24
@@ -104,7 +103,6 @@
     barrier = pltpu.get_barrier_semaphore()
     for d in (8, 7, 9, 6, 10, 5, 11, 4, 12, 3, 13, 2, 14, 15):
         pl.when(z + d < PLANES)(lambda d=d: tell(barrier, seq=seq + d * PLANE))
-        pl.when((z - d >= 0) & (z - d < EARLY))(lambda d=d: tell(barrier, seq=seq - d * PLANE))
     for t in heads:
         tell(barrier, head=t)
     for t in plane:
@@ -118,8 +116,7 @@
 
     above = (z + 1 < PLANES).astype(jnp.int32)
     below = (z > 0).astype(jnp.int32)
-    partners = len(plane) + len(heads) + PLANE * (above + below)
-    partners += jnp.where(z < EARLY, PLANES - 1 - above - below, z - below)
+    partners = len(plane) + len(heads) + PLANE * (above + below) + z - below
 
     def send(src, dst, group, to):
         pltpu.make_async_remote_copy(
@@ -157,8 +154,8 @@
         (Z6, 2, sixths, valid6, (1, 0, 2)),
         (Z5, 1, fifths, valid5, (1, 0, 2)),
     )
-    def each_group(ready):
-        for group, size, others, valid, slots in classes:
+    def each_group(ready, chosen):
+        for group, size, others, valid, slots in chosen:
             for i, (other, ok, slot) in enumerate(zip(others, valid, slots, strict=True)):
                 targets = [(other * size + (z % size ^ e)) * PLANE + r for e in range(size)]
 
@@ -175,17 +172,19 @@
 
                 ready(ok, other * size, push, admit, await_open)
 
-    def first_packets(ok, low, push, admit, await_open):
-        pl.when(ok & ((low < z) | (z < EARLY)))(push)
-        pl.when(ok & (low < z) & (low >= EARLY))(admit)
-
-    def later_packets(ok, low, push, admit, await_open):
-        @pl.when(ok & (low > z) & (z >= EARLY))
+    def to_lower(ok, low, push, admit, await_open):
+        @pl.when(ok & (low < z))
+        def _():
+            push()
+            admit()
+
+    def to_higher(ok, low, push, admit, await_open):
+        @pl.when(ok & (low > z))
         def _():
             await_open()
             push()
 
-    each_group(first_packets)
+    each_group(to_lower, classes)
 
     def packets(wait, which):
         group, size, _, valid, slots = classes[which]
@@ -255,8 +254,7 @@
     put(0, LEAF, kv[0])
     put(1, 0, kv[0])
 
-    each_group(later_packets)
-
+    each_group(to_higher, (classes[2], classes[1], classes[0]))
     packets(arrived, 2)
     packets(arrived, 1)
     mean = group_mean(64)

time: 35.8 us -> 34 us (0.950)
  the two profiles are of different devices: /device:TPU:32 before, /device:TPU:1 now
where the time goes in v3:
time: 34 us; the launch traced here: 33.9 us
  Pallas kernels  32.4 us (95%)
  local copies, waits for them, and re-layouts  1.47 us (4%)
    pallas_call x1, Pallas kernels, shards(): pl.pallas_call(kernel, out_shape=jax.ShapeDtypeStruct((64, 512), bf16), i...  32.4 us
    unnamed x1, local copies, waits for them, and re-layouts  1.47 us

profile of v3, /device:TPU:1, one launch (start us, length us, event | category | flops | bytes accessed | tf_op | source)
XLA Modules:
  0.0 33.9 jit_solution(5530368582556920481)
XLA Ops:
  0.0 32.4 %shard_map.46 = bf16[64,512]{1,0:T(8,128)(2,1)} custom-call(bf16[256,128]{1,0:T(8,128)(2,1)} %q_hbm.1, bf16[256,128]{1,0:T(8,128)(2,1)} %k_hbm.1, bf16[256,128]{1,0:T(8,128)(2,1)} %v_hbm.1, bf16[512,512]{1,0:T(8,128)(2,1)} %w_hbm.1), custom_call_target="tpu_custom_call" | custom-call | tf_op jit(solution)/shard_map/pallas_call | solution.py:359
  32.4 1.5 %copy.6 = bf16[64,512]{1,0:T(8,128)(2,1)} copy(bf16[64,512]{1,0:T(8,128)(2,1)} %shard_map.46) | data formatting | bytes 131072

commit v4 on v3

--- a/solution.py
+++ b/solution.py
@@ -63,7 +63,7 @@
     q_hbm, k_hbm, v_hbm, w_hbm, out_ref,
     q, kv, w, s1, s2, s3, s4, n0, n1, r2, r3, r4, zbuf, pmid, pfar,
     qm, scores, probs, total, att, gath,
-    local_sem, send_sem, recv_sem, open_sem,
+    local_sem, send_sem, recv_sem, open_sem, open_near, open_head,
 ):
     seq = lax.axis_index("seq")
     head = lax.axis_index("head")
@@ -97,26 +97,42 @@
         for ref in (n0, n1, r2, r3, r4):
             ref[...] = jnp.zeros_like(ref)
 
+    def rank(place):
+        return (place >> 1 ^ place >> 2) * 2 + (place & 1)
+
     def tell(sem, **to):
         pl.semaphore_signal(sem, inc=1, device_id=to, device_id_type=MESH)
 
     barrier = pltpu.get_barrier_semaphore()
     for d in (8, 7, 9, 6, 10, 5, 11, 4, 12, 3, 13, 2, 14, 15):
         pl.when(z + d < PLANES)(lambda d=d: tell(barrier, seq=seq + d * PLANE))
-    for t in heads:
-        tell(barrier, head=t)
-    for t in plane:
-        tell(barrier, seq=t)
-    for d in (1, -1):
-
-        @pl.when((z + d >= 0) & (z + d < PLANES))
-        def _(d=d):
-            for e in range(PLANE):
-                tell(barrier, seq=(z + d) * PLANE + (r ^ e))
-
+    mine, mine_head = rank(r), head ^ head >> 1
     above = (z + 1 < PLANES).astype(jnp.int32)
     below = (z > 0).astype(jnp.int32)
-    partners = len(plane) + len(heads) + PLANE * (above + below) + z - below
+
+    def greet(later, near, heads_sem):
+        def chosen(a, b):
+            return a < b if later else a > b
+
+        for t in heads:
+            pl.when(chosen(mine_head, t ^ t >> 1))(lambda t=t: tell(heads_sem, head=t))
+        for d in (0, 1, -1):
+            for e in range(1, PLANE):
+                place = r ^ e
+
+                if d == 0 and e == 1:
+                    if later:
+                        tell(near, seq=seq ^ 1)
+                    continue
+
+                @pl.when((z + d >= 0) & (z + d < PLANES) & chosen(mine, rank(place)))
+                def _(d=d, place=place):
+                    tell(near, seq=(z + d) * PLANE + place)
+
+        d = 1 if later else -1
+        pl.when((z + d >= 0) & (z + d < PLANES))(lambda: tell(near, seq=seq + d * PLANE))
+
+    greet(True, barrier, barrier)
 
     def send(src, dst, group, to):
         pltpu.make_async_remote_copy(
@@ -142,7 +158,8 @@
     last = dot(mean[:8, :16], level)
     zbuf[z] = jnp.concatenate([last[:, :128], last[:, 128:]], axis=0).astype(jnp.bfloat16)
 
-    pl.semaphore_wait(barrier, partners)
+    core = seq % 2
+    pl.semaphore_wait(barrier, mine * (1 + above + below) - core + 1 + z + mine_head)
 
     seventh = z // 4
     step = 3 - 6 * (seventh % 2)
@@ -185,6 +202,7 @@
             push()
 
     each_group(to_lower, classes)
+    greet(False, open_near, open_head)
 
     def packets(wait, which):
         group, size, _, valid, slots = classes[which]
@@ -205,6 +223,9 @@
             dst[0, side] = half.astype(jnp.bfloat16)
         for e, t in enumerate(plane):
             send(dst.at[0], dst.at[e + 1], group, {"seq": t})
+
+    later_near = (PLANE - 1 - mine) * (1 + above + below) - 1 + core + above
+    pl.when(later_near > 0)(lambda: pl.semaphore_wait(open_near, later_near))
 
     has_prev, has_next = seq >= 1, seq + 1 < SEQ
     chain = ((L2, 1, s2, r2), (L3, 2, s3, r3), (L4, 4, s4, r4))
@@ -293,12 +314,6 @@
     put(0, NEAR + MID, keys, row)
     put(1, NEAR + MID, keys, row)
 
-    for low in range(0, ROWS, STRIP):
-        strip = scores[low : low + STRIP]
-        weights = jnp.exp(strip - jnp.max(strip, axis=1, keepdims=True))
-        total[low : low + STRIP] = jnp.sum(weights, axis=1, keepdims=True)
-        probs[low : low + STRIP] = weights.astype(jnp.bfloat16)
-
     second = r2[:, 1].reshape(192, LEAF)
     middle = jnp.concatenate([r3[:, 1].reshape(192, LEAF), r4[:, 1].reshape(192, LEAF)], axis=0)
     far = [pmid[:, 1].reshape(MID, LEAF), pfar[:, 1].reshape(FAR, LEAF)]
@@ -306,17 +321,24 @@
         (n0[0, 1], kv[1], n1[0, 1, :64], n1[1, 1], second, middle, *far),
         (kv[1], n0[1, 1], n1[0, 1], n1[1, 1, 64:], second, middle, *far),
     )
+    later_heads = HEADS_DEV - 1 - mine_head
+    pl.when(later_heads > 0)(lambda: pl.semaphore_wait(open_head, later_heads))
     for leaf in range(2):
         rows = slice(leaf * SPAN, (leaf + 1) * SPAN)
+        for low in range(leaf * SPAN, (leaf + 1) * SPAN, STRIP):
+            strip = scores[low : low + STRIP]
+            weights = jnp.exp(strip - jnp.max(strip, axis=1, keepdims=True))
+            total[low : low + STRIP] = jnp.sum(weights, axis=1, keepdims=True)
+            probs[low : low + STRIP] = weights.astype(jnp.bfloat16)
         numer = dot(probs[rows], jnp.concatenate(near[leaf], axis=0))
         numer = numer / total[rows]
         rows_out = jnp.where(lane < HD, numer[:LEAF], numer[LEAF:]).astype(jnp.bfloat16)
         att[2 * leaf] = rows_out[:64]
         att[2 * leaf + 1] = rows_out[64:]
+        for to in (2 * leaf, 2 * leaf + 1):
+            pl.when(head != to)(lambda to=to: send(att.at[to], gath.at[head], AT, {"head": to}))
 
     gath[head] = att[head]
-    for t in heads:
-        send(att.at[t], gath.at[head], AT, {"head": t})
     loads[3].wait()
     arrived(gath.at[pl.ds(0, HEADS_DEV - 1)], AT)
     rows = jnp.concatenate([gath[i] for i in range(HEADS_DEV)], axis=1)
@@ -367,6 +389,8 @@
             pltpu.SemaphoreType.DMA((GROUPS,)),
             pltpu.SemaphoreType.DMA((GROUPS,)),
             pltpu.SemaphoreType.REGULAR((GROUPS - Z5,)),
+            pltpu.SemaphoreType.REGULAR,
+            pltpu.SemaphoreType.REGULAR,
         ],
         compiler_params=pltpu.CompilerParams(
             collective_id=0, has_side_effects=True, vmem_limit_bytes=63_400_000

time: 34 us -> 33.2 us (0.976)
  Pallas kernels: 32.4 us -> 31.6 us
    pallas_call x1, Pallas kernels: 32.4 us -> 31.6 us  [shards(): pl.pallas_call(kernel, out_shape=jax.ShapeDtypeStruct((64, 512), bf16), i...]
where the time goes in v4:
time: 33.2 us; the launch traced here: 33 us
  Pallas kernels  31.6 us (95%)
  local copies, waits for them, and re-layouts  1.47 us (4%)
    pallas_call x1, Pallas kernels, shards(): pl.pallas_call(kernel, out_shape=jax.ShapeDtypeStruct((64, 512), bf16), i...  31.6 us
    unnamed x1, local copies, waits for them, and re-layouts  1.47 us

profile of v4, /device:TPU:1, one launch (start us, length us, event | category | flops | bytes accessed | tf_op | source)
XLA Modules:
  0.0 33.0 jit_solution(16606533626748259585)
XLA Ops:
  0.0 31.6 %shard_map.46 = bf16[64,512]{1,0:T(8,128)(2,1)} custom-call(bf16[256,128]{1,0:T(8,128)(2,1)} %q_hbm.1, bf16[256,128]{1,0:T(8,128)(2,1)} %k_hbm.1, bf16[256,128]{1,0:T(8,128)(2,1)} %v_hbm.1, bf16[512,512]{1,0:T(8,128)(2,1)} %w_hbm.1), custom_call_target="tpu_custom_call" | custom-call | tf_op jit(solution)/shard_map/pallas_call | solution.py:381
  31.6 1.5 %copy.6 = bf16[64,512]{1,0:T(8,128)(2,1)} copy(bf16[64,512]{1,0:T(8,128)(2,1)} %shard_map.46) | data formatting | bytes 131072

commit v5 on v4

--- a/solution.py
+++ b/solution.py
@@ -91,6 +91,7 @@
     heads = [head ^ e for e in (2, 1, 3)]
 
     zbuf[...] = jnp.zeros_like(zbuf)
+    pmid[:, 2] = jnp.zeros_like(pmid[:, 2])
 
     @pl.when((z == 0) | (z == PLANES - 1))
     def _():
@@ -165,15 +166,25 @@
     step = 3 - 6 * (seventh % 2)
     sevenths = [(seventh + 2) % 4, jnp.clip(seventh + step, 0, 3)]
     valid7 = [seventh >= 0, (seventh + step >= 0) & (seventh + step < 4)]
-    (sixths, valid6), (fifths, valid5) = groups(2 * PLANE), groups(PLANE)
+    low_half = z < PLANES // 2
+
+    def existing_first(size):
+        (a, b, c), (is_a, is_b, is_c) = groups(size)
+        pick = lambda low, high: jnp.where(low_half, low, high)
+        others, valid = [pick(b, a), c, pick(a, b)], [pick(is_b, is_a), is_c, pick(is_a, is_b)]
+        return others, valid
+
+    (sixths, valid6), (fifths, valid5) = existing_first(2 * PLANE), existing_first(PLANE)
+    one = low_half.astype(jnp.int32)
+    here, there = (one, 2, 1 - one), (1 - one, 2, one)
     classes = (
-        (Z7, 4, sevenths, valid7, (0, 1)),
-        (Z6, 2, sixths, valid6, (1, 0, 2)),
-        (Z5, 1, fifths, valid5, (1, 0, 2)),
+        (Z7, 4, sevenths, valid7, (0, 1), (0, 1)),
+        (Z6, 2, sixths, valid6, here, there),
+        (Z5, 1, fifths, valid5, here, there),
     )
     def each_group(ready, chosen):
-        for group, size, others, valid, slots in chosen:
-            for i, (other, ok, slot) in enumerate(zip(others, valid, slots, strict=True)):
+        for group, size, others, valid, places, slots in chosen:
+            for other, ok, i, slot in zip(others, valid, places, slots, strict=True):
                 targets = [(other * size + (z % size ^ e)) * PLANE + r for e in range(size)]
 
                 def push(targets=targets, group=group, slot=slot):
@@ -205,24 +216,26 @@
     greet(False, open_near, open_head)
 
     def packets(wait, which):
-        group, size, _, valid, slots = classes[which]
-        for i, ok in enumerate(valid):
-            slot = slots[i] if wait is sent else i
+        group, size, _, valid, places, slots = classes[which]
+        for ok, slot in zip(valid, slots if wait is sent else places, strict=True):
             pl.when(ok)(lambda slot=slot: wait(zbuf.at[pl.ds(0, size)], group + slot))
 
     def gathered(which):
-        _, size, others, valid, _ = classes[which]
+        _, size, others, valid, _, _ = classes[which]
         picks = [jnp.where(ok, other, z // size) for other, ok in zip(others, valid, strict=True)]
         rows = [zbuf[pl.ds(g * size, size)].reshape(size * 16, LEAF) for g in picks]
         return jnp.concatenate(rows, axis=0)
 
-    def forward(rows, dst, group):
-        rows = rows.reshape(rows.shape[0] // 16, 2, 8, LEAF)
+    def forward(blocks, dst):
         for side in range(2):
-            half = jnp.concatenate([rows[i, side] for i in range(rows.shape[0])], axis=0)
-            dst[0, side] = half.astype(jnp.bfloat16)
-        for e, t in enumerate(plane):
-            send(dst.at[0], dst.at[e + 1], group, {"seq": t})
+            half = slice(side * 8, side * 8 + 8)
+            dst[side] = jnp.concatenate([block[half] for block in blocks], axis=0).astype(jnp.bfloat16)
+
+    ends = (z < 2) | (z >= PLANES - 2)
+
+    def middle_blocks(wait):
+        pl.when(ends)(lambda: wait(pmid.at[pl.ds(0, PLANE - 1), pl.ds(0, 2)], PM))
+        pl.when(jnp.logical_not(ends))(lambda: wait(pmid.at[pl.ds(0, PLANE - 1)], PM))
 
     later_near = (PLANE - 1 - mine) * (1 + above + below) - 1 + core + above
     pl.when(later_near > 0)(lambda: pl.semaphore_wait(open_near, later_near))
@@ -280,11 +293,24 @@
     packets(arrived, 1)
     mean = group_mean(64)
     sixth = dot(mean[:48, :96], gathered(1))
-    forward(jnp.concatenate([gathered(2).astype(jnp.float32), sixth], axis=0), pmid, PM)
+    fifth = gathered(2).astype(jnp.float32)
+    for i in range(3):
+        group = slice(i * 16, i * 16 + 16)
+        forward((fifth[group], sixth[group]), pmid.at[0, i])
+
+    def to_plane(count):
+        for e, t in enumerate(plane):
+            send(pmid.at[0, pl.ds(0, count)], pmid.at[e + 1, pl.ds(0, count)], PM, {"seq": t})
+
+    pl.when(ends)(lambda: to_plane(2))
+    pl.when(jnp.logical_not(ends))(lambda: to_plane(3))
 
     packets(arrived, 0)
     sixth = dot(mean, gathered(0)).astype(jnp.bfloat16)
-    forward(dot(mean[:32, :64], sixth), pfar, PF)
+    last = dot(mean[:32, :64], sixth)
+    forward((last[:16], last[16:]), pfar.at[0])
+    for e, t in enumerate(plane):
+        send(pfar.at[0], pfar.at[e + 1], PF, {"seq": t})
 
     bias_prev, bias_next = open_if(has_prev), open_if(has_next)
     bias2 = [(64, open_if(ok)) for ok in groups(1)[1]]
@@ -302,10 +328,10 @@
     put(0, 768, keys, row)
     put(1, 768, keys, row)
 
-    biases = [(8, open_if(ok)) for ok in [*valid5, *valid6]]
+    biases = [(8, open_if(ok)) for pair in zip(valid5, valid6, strict=True) for ok in pair]
     row = bias_row(biases * PLANE)
-    arrived(pmid.at[pl.ds(0, PLANE - 1)], PM)
-    keys = pmid[:, 0].reshape(MID, LEAF)
+    middle_blocks(arrived)
+    keys = pmid[:, :, 0].reshape(MID, LEAF)
     put(0, NEAR, keys, row)
     put(1, NEAR, keys, row)
     row = bias_row([(8, open_if(ok)) for ok in valid7] * PLANE)
@@ -316,7 +342,7 @@
 
     second = r2[:, 1].reshape(192, LEAF)
     middle = jnp.concatenate([r3[:, 1].reshape(192, LEAF), r4[:, 1].reshape(192, LEAF)], axis=0)
-    far = [pmid[:, 1].reshape(MID, LEAF), pfar[:, 1].reshape(FAR, LEAF)]
+    far = [pmid[:, :, 1].reshape(MID, LEAF), pfar[:, 1].reshape(FAR, LEAF)]
     near = (
         (n0[0, 1], kv[1], n1[0, 1, :64], n1[1, 1], second, middle, *far),
         (kv[1], n0[1, 1], n1[0, 1], n1[1, 1, 64:], second, middle, *far),
@@ -347,7 +373,7 @@
     for which in range(3):
         packets(sent, which)
     near_done(sent, 1, (1, 0, 2))
-    sent(pmid.at[pl.ds(0, PLANE - 1)], PM)
+    middle_blocks(sent)
     sent(pfar.at[pl.ds(0, PLANE - 1)], PF)
     sent(gath.at[pl.ds(0, HEADS_DEV - 1)], AT)
 
@@ -369,7 +395,7 @@
         ((6, 2, 32, LEAF), bf16),
         ((12, 2, 16, LEAF), bf16),
         ((PLANES, 16, LEAF), bf16),
-        ((PLANE, 2, 48, LEAF), bf16),
+        ((PLANE, 3, 2, 16, LEAF), bf16),
         ((PLANE, 2, 16, LEAF), bf16),
         ((2, SPAN, LEAF), bf16),
         ((ROWS, COLS), f32),

time: 33.2 us -> 32.6 us (0.982)
  Pallas kernels: 31.6 us -> 31 us
    pallas_call x1, Pallas kernels: 31.6 us -> 31 us  [shards(): pl.pallas_call(kernel, out_shape=jax.ShapeDtypeStruct((64, 512), bf16), i...]
where the time goes in v5:
time: 32.6 us; the launch traced here: 32.5 us
  Pallas kernels  31 us (95%)
  local copies, waits for them, and re-layouts  1.47 us (5%)
    pallas_call x1, Pallas kernels, shards(): pl.pallas_call(kernel, out_shape=jax.ShapeDtypeStruct((64, 512), bf16), i...  31 us
    unnamed x1, local copies, waits for them, and re-layouts  1.47 us

profile of v5, /device:TPU:1, one launch (start us, length us, event | category | flops | bytes accessed | tf_op | source)
XLA Modules:
  0.0 32.5 jit_solution(7065197359151884997)
XLA Ops:
  0.0 31.0 %shard_map.46 = bf16[64,512]{1,0:T(8,128)(2,1)} custom-call(bf16[256,128]{1,0:T(8,128)(2,1)} %q_hbm.1, bf16[256,128]{1,0:T(8,128)(2,1)} %k_hbm.1, bf16[256,128]{1,0:T(8,128)(2,1)} %v_hbm.1, bf16[512,512]{1,0:T(8,128)(2,1)} %w_hbm.1), custom_call_target="tpu_custom_call" | custom-call | tf_op jit(solution)/shard_map/pallas_call | solution.py:407
  31.0 1.5 %copy.6 = bf16[64,512]{1,0:T(8,128)(2,1)} copy(bf16[64,512]{1,0:T(8,128)(2,1)} %shard_map.46) | data formatting | bytes 131072

commit v6 on v5

--- a/solution.py
+++ b/solution.py
@@ -117,21 +117,23 @@
 
         for t in heads:
             pl.when(chosen(mine_head, t ^ t >> 1))(lambda t=t: tell(heads_sem, head=t))
-        for d in (0, 1, -1):
-            for e in range(1, PLANE):
+        for e in range(1, PLANE):
+            if e > 1:
+                pl.when(chosen(mine, rank(r ^ e)))(lambda e=e: tell(near, seq=seq ^ e))
+            elif later:
+                tell(near, seq=seq ^ e)
+        for d in (1, -1):
+            for e in range(PLANE):
                 place = r ^ e
-
-                if d == 0 and e == 1:
-                    if later:
-                        tell(near, seq=seq ^ 1)
-                    continue
-
-                @pl.when((z + d >= 0) & (z + d < PLANES) & chosen(mine, rank(place)))
+                if d == 1:
+                    first = jnp.logical_not((place < 2) & (r >= 2))
+                else:
+                    first = (r < 2) & (place >= 2)
+                turn = first if later else jnp.logical_not(first)
+
+                @pl.when((z + d >= 0) & (z + d < PLANES) & turn)
                 def _(d=d, place=place):
                     tell(near, seq=(z + d) * PLANE + place)
-
-        d = 1 if later else -1
-        pl.when((z + d >= 0) & (z + d < PLANES))(lambda: tell(near, seq=seq + d * PLANE))
 
     greet(True, barrier, barrier)
 
@@ -160,7 +162,9 @@
     zbuf[z] = jnp.concatenate([last[:, :128], last[:, 128:]], axis=0).astype(jnp.bfloat16)
 
     core = seq % 2
-    pl.semaphore_wait(barrier, mine * (1 + above + below) - core + 1 + z + mine_head)
+    inner = (r >= 2).astype(jnp.int32)
+    early_beside = 2 * inner * above + (2 + 6 * inner) * below
+    pl.semaphore_wait(barrier, mine - core + 1 + early_beside + z - below + mine_head)
 
     seventh = z // 4
     step = 3 - 6 * (seventh % 2)
@@ -237,7 +241,7 @@
         pl.when(ends)(lambda: wait(pmid.at[pl.ds(0, PLANE - 1), pl.ds(0, 2)], PM))
         pl.when(jnp.logical_not(ends))(lambda: wait(pmid.at[pl.ds(0, PLANE - 1)], PM))
 
-    later_near = (PLANE - 1 - mine) * (1 + above + below) - 1 + core + above
+    later_near = PLANE - 2 - mine + core + PLANE * (above + below) - early_beside
     pl.when(later_near > 0)(lambda: pl.semaphore_wait(open_near, later_near))
 
     has_prev, has_next = seq >= 1, seq + 1 < SEQ

time: 32.6 us -> 32.4 us (level)
  no operation moved by 1% of the time
where the time goes in v6:
time: 32.4 us; the launch traced here: 32.2 us
  Pallas kernels  30.7 us (95%)
  local copies, waits for them, and re-layouts  1.47 us (5%)
    pallas_call x1, Pallas kernels, shards(): pl.pallas_call(kernel, out_shape=jax.ShapeDtypeStruct((64, 512), bf16), i...  30.7 us
    unnamed x1, local copies, waits for them, and re-layouts  1.47 us

profile of v6, /device:TPU:1, one launch (start us, length us, event | category | flops | bytes accessed | tf_op | source)
XLA Modules:
  0.0 32.2 jit_solution(12300060363928510902)
XLA Ops:
  0.0 30.7 %shard_map.46 = bf16[64,512]{1,0:T(8,128)(2,1)} custom-call(bf16[256,128]{1,0:T(8,128)(2,1)} %q_hbm.1, bf16[256,128]{1,0:T(8,128)(2,1)} %k_hbm.1, bf16[256,128]{1,0:T(8,128)(2,1)} %v_hbm.1, bf16[512,512]{1,0:T(8,128)(2,1)} %w_hbm.1), custom_call_target="tpu_custom_call" | custom-call | tf_op jit(solution)/shard_map/pallas_call | solution.py:411
  30.7 1.5 %copy.6 = bf16[64,512]{1,0:T(8,128)(2,1)} copy(bf16[64,512]{1,0:T(8,128)(2,1)} %shard_map.46) | data formatting | bytes 131072

commit v7 on v6

--- a/solution.py
+++ b/solution.py
@@ -62,7 +62,7 @@
 def kernel(
     q_hbm, k_hbm, v_hbm, w_hbm, out_ref,
     q, kv, w, s1, s2, s3, s4, n0, n1, r2, r3, r4, zbuf, pmid, pfar,
-    qm, scores, probs, total, att, gath,
+    qm, scores, top, probs, total, att, gath,
     local_sem, send_sem, recv_sem, open_sem, open_near, open_head,
 ):
     seq = lax.axis_index("seq")
@@ -338,11 +338,14 @@
     keys = pmid[:, :, 0].reshape(MID, LEAF)
     put(0, NEAR, keys, row)
     put(1, NEAR, keys, row)
+    for low in range(0, ROWS, STRIP):
+        parts = [scores[low : low + STRIP, at : at + LEAF] for at in range(0, NEAR + MID, LEAF)]
+        while len(parts) > 1:
+            parts = [jnp.maximum(*parts[i : i + 2]) if i + 1 < len(parts) else parts[i] for i in range(0, len(parts), 2)]
+        top[low : low + STRIP] = parts[0]
     row = bias_row([(8, open_if(ok)) for ok in valid7] * PLANE)
     arrived(pfar.at[pl.ds(0, PLANE - 1)], PF)
     keys = pfar[:, 0].reshape(FAR, LEAF)
-    put(0, NEAR + MID, keys, row)
-    put(1, NEAR + MID, keys, row)
 
     second = r2[:, 1].reshape(192, LEAF)
     middle = jnp.concatenate([r3[:, 1].reshape(192, LEAF), r4[:, 1].reshape(192, LEAF)], axis=0)
@@ -354,10 +357,12 @@
     later_heads = HEADS_DEV - 1 - mine_head
     pl.when(later_heads > 0)(lambda: pl.semaphore_wait(open_head, later_heads))
     for leaf in range(2):
+        put(leaf, NEAR + MID, keys, row)
         rows = slice(leaf * SPAN, (leaf + 1) * SPAN)
         for low in range(leaf * SPAN, (leaf + 1) * SPAN, STRIP):
             strip = scores[low : low + STRIP]
-            weights = jnp.exp(strip - jnp.max(strip, axis=1, keepdims=True))
+            highest = jnp.maximum(top[low : low + STRIP], strip[:, NEAR + MID :])
+            weights = jnp.exp(strip - jnp.max(highest, axis=1, keepdims=True))
             total[low : low + STRIP] = jnp.sum(weights, axis=1, keepdims=True)
             probs[low : low + STRIP] = weights.astype(jnp.bfloat16)
         numer = dot(probs[rows], jnp.concatenate(near[leaf], axis=0))
@@ -403,6 +408,7 @@
         ((PLANE, 2, 16, LEAF), bf16),
         ((2, SPAN, LEAF), bf16),
         ((ROWS, COLS), f32),
+        ((ROWS, LEAF), f32),
         ((ROWS, COLS), bf16),
         ((ROWS, 1), f32),
         ((HEADS_DEV, 64, LEAF), bf16),

time: 32.4 us -> 32.3 us (level)
  no operation moved by 1% of the time
where the time goes in v7:
time: 32.3 us; the launch traced here: 32.2 us
  Pallas kernels  30.7 us (95%)
  local copies, waits for them, and re-layouts  1.47 us (5%)
    pallas_call x1, Pallas kernels, shards(): pl.pallas_call(kernel, out_shape=jax.ShapeDtypeStruct((64, 512), bf16), i...  30.7 us
    unnamed x1, local copies, waits for them, and re-layouts  1.47 us

profile of v7, /device:TPU:1, one launch (start us, length us, event | category | flops | bytes accessed | tf_op | source)
XLA Modules:
  0.0 32.2 jit_solution(15516358725049461525)
XLA Ops:
  0.0 30.7 %shard_map.46 = bf16[64,512]{1,0:T(8,128)(2,1)} custom-call(bf16[256,128]{1,0:T(8,128)(2,1)} %q_hbm.1, bf16[256,128]{1,0:T(8,128)(2,1)} %k_hbm.1, bf16[256,128]{1,0:T(8,128)(2,1)} %v_hbm.1, bf16[512,512]{1,0:T(8,128)(2,1)} %w_hbm.1), custom_call_target="tpu_custom_call" | custom-call | tf_op jit(solution)/shard_map/pallas_call | solution.py:417
  30.7 1.5 %copy.6 = bf16[64,512]{1,0:T(8,128)(2,1)} copy(bf16[64,512]{1,0:T(8,128)(2,1)} %shard_map.46) | data formatting | bytes 131072

commit v8 on v6

--- a/solution.py
+++ b/solution.py
@@ -207,8 +207,8 @@
     def to_lower(ok, low, push, admit, await_open):
         @pl.when(ok & (low < z))
         def _():
+            admit()
             push()
-            admit()
 
     def to_higher(ok, low, push, admit, await_open):
         @pl.when(ok & (low > z))
@@ -341,8 +341,6 @@
     row = bias_row([(8, open_if(ok)) for ok in valid7] * PLANE)
     arrived(pfar.at[pl.ds(0, PLANE - 1)], PF)
     keys = pfar[:, 0].reshape(FAR, LEAF)
-    put(0, NEAR + MID, keys, row)
-    put(1, NEAR + MID, keys, row)
 
     second = r2[:, 1].reshape(192, LEAF)
     middle = jnp.concatenate([r3[:, 1].reshape(192, LEAF), r4[:, 1].reshape(192, LEAF)], axis=0)
@@ -354,6 +352,7 @@
     later_heads = HEADS_DEV - 1 - mine_head
     pl.when(later_heads > 0)(lambda: pl.semaphore_wait(open_head, later_heads))
     for leaf in range(2):
+        put(leaf, NEAR + MID, keys, row)
         rows = slice(leaf * SPAN, (leaf + 1) * SPAN)
         for low in range(leaf * SPAN, (leaf + 1) * SPAN, STRIP):
             strip = scores[low : low + STRIP]

time: 32.4 us -> 32.3 us (level)
  no operation moved by 1% of the time
where the time goes in v8:
time: 32.3 us; the launch traced here: 32.2 us
  Pallas kernels  30.7 us (95%)
  local copies, waits for them, and re-layouts  1.47 us (5%)
    pallas_call x1, Pallas kernels, shards(): pl.pallas_call(kernel, out_shape=jax.ShapeDtypeStruct((64, 512), bf16), i...  30.7 us
    unnamed x1, local copies, waits for them, and re-layouts  1.47 us

profile of v8, /device:TPU:1, one launch (start us, length us, event | category | flops | bytes accessed | tf_op | source)
XLA Modules:
  0.0 32.2 jit_solution(3958064322109959263)
XLA Ops:
  0.0 30.7 %shard_map.46 = bf16[64,512]{1,0:T(8,128)(2,1)} custom-call(bf16[256,128]{1,0:T(8,128)(2,1)} %q_hbm.1, bf16[256,128]{1,0:T(8,128)(2,1)} %k_hbm.1, bf16[256,128]{1,0:T(8,128)(2,1)} %v_hbm.1, bf16[512,512]{1,0:T(8,128)(2,1)} %w_hbm.1), custom_call_target="tpu_custom_call" | custom-call | tf_op jit(solution)/shard_map/pallas_call | solution.py:410
  30.7 1.5 %copy.6 = bf16[64,512]{1,0:T(8,128)(2,1)} copy(bf16[64,512]{1,0:T(8,128)(2,1)} %shard_map.46) | data formatting | bytes 131072
